TPU v7x, 256 devices: a whole 4x4x8 slice. The times are simulated.
256 devices in a mesh: dp: 32 (over y, z), tensor: 8 (over x, core).
Axes of the slice: x: 4, y: 4, z: 8, core: 2. Of those that a mesh axis runs over, the one named last changes fastest.
Arguments:
- momentum: bfloat16 [8192, 28672], P('dp', 'tensor'), may hold values from -6 to 6
- grad: bfloat16 [8192, 28672], P('dp', 'tensor'), may hold values from -70 to 70
- basis: float32 [1024, 28672], P('dp', 'tensor'), may hold values from -6 to 6
Outputs:
- update: bfloat16 [8192, 28672], P('dp', 'tensor')
- new_momentum: bfloat16 [8192, 28672], P('dp', 'tensor')
- new_basis: float32 [1024, 28672], P('dp', 'tensor')
All inputs are finite; a program needn't handle non-finite values.
Results may differ from a plain program's by a relative error of at most 0.024.
Values may be sent and summed in bfloat16 or wider, within the bound.
No kernel may reach another device: no remote copies, remote signals or barrier semaphores. Data moves between devices by JAX's collectives and lax.ppermute only.
A program may use at most 128 MiB of HBM per device.

v0:
```python
import math

import jax
import jax.numpy as jnp
from jax import lax
from jax.sharding import PartitionSpec as P

D = 8192
FF = 28672
R = 1024


MOMENTUM = 0.95
JITTER = 0.001
NORM_EPS = 1e-08


def gram_of(factor):
    return jnp.dot(
        factor.T, factor, precision=lax.Precision.HIGHEST, preferred_element_type=jnp.float32
    )


def inverse_factor(gram_matrix):
    order_size = gram_matrix.shape[0]
    identity = jnp.eye(order_size, dtype=jnp.float32)
    shifted = gram_matrix + JITTER * jnp.trace(gram_matrix) / order_size * identity
    lower_factor = jnp.linalg.cholesky(shifted)
    return jax.scipy.linalg.solve_triangular(lower_factor, identity, lower=True)


def orthonormalize(sketch, gram_matrix):
    return jnp.dot(
        sketch,
        inverse_factor(gram_matrix).T,
        precision=lax.Precision.HIGHEST,
        preferred_element_type=jnp.float32,
    ).astype(jnp.bfloat16)


def per_device(momentum, grad, basis):
    summed = (momentum.astype(jnp.float32) + grad.astype(jnp.float32)).astype(jnp.bfloat16)
    summed = lax.optimization_barrier(summed)
    narrow_basis = basis.astype(jnp.bfloat16)
    local_rows = momentum.shape[0]
    rank_rows = basis.shape[0]
    full_basis = lax.all_gather(narrow_basis, "dp", axis=0, tiled=True)
    partial_sketch = lax.dot_general(
        summed, full_basis, (((1,), (1,)), ((), ())), preferred_element_type=jnp.float32
    )
    sketch = lax.psum(partial_sketch, "tensor")
    gram_matrix = lax.psum(gram_of(sketch), "dp")
    orthonormal = orthonormalize(sketch, gram_matrix)
    rank_total = orthonormal.shape[1]
    update_scale = math.sqrt(D * FF / R)
    coefficients = lax.psum_scatter(
        lax.dot_general(
            orthonormal, summed, (((0,), (0,)), ((), ())), preferred_element_type=jnp.float32
        ).astype(jnp.bfloat16),
        "dp",
        scatter_dimension=0,
        tiled=True,
    ).astype(jnp.float32)
    squares = jnp.sum(coefficients * coefficients, axis=1)
    own_start = lax.axis_index("dp") * rank_rows
    placed = lax.dynamic_update_slice_in_dim(
        jnp.zeros((rank_total,), jnp.float32), squares, own_start, 0
    )
    column_norms = jnp.sqrt(lax.psum(placed, ("dp", "tensor"))) + NORM_EPS
    scaling = update_scale / column_norms
    stacked = jnp.concatenate(
        [orthonormal, (orthonormal.astype(jnp.float32) * scaling[None, :]).astype(jnp.bfloat16)],
        axis=0,
    )
    all_coefficients = lax.all_gather(coefficients.astype(jnp.bfloat16), "dp", axis=0, tiled=True)
    products = jnp.dot(stacked, all_coefficients, preferred_element_type=jnp.float32)
    own_norms = lax.dynamic_slice_in_dim(column_norms, own_start, rank_rows, 0)
    new_basis = math.sqrt(FF) * coefficients / own_norms[:, None]
    feedback = products[:local_rows]
    update = products[local_rows:].astype(jnp.bfloat16)
    new_momentum = (summed.astype(jnp.float32) - (1.0 - MOMENTUM) * feedback).astype(jnp.bfloat16)
    return (update, new_momentum, new_basis)


def solution(mesh):
    in_specs = (P("dp", "tensor"), P("dp", "tensor"), P("dp", "tensor"))
    out_specs = (P("dp", "tensor"), P("dp", "tensor"), P("dp", "tensor"))
    return jax.shard_map(
        per_device, mesh=mesh, in_specs=in_specs, out_specs=out_specs, check_vma=False
    )
```

profile of v0, /device:TPU:1, one launch (start us, length us, event | category | flops | bytes accessed | tf_op | source)
XLA Modules:
  0.0 1071.3 jit_solution(10124754990401175949)
XLA Ops:
  11.5 96.4 %all-gather.3.cloned.1.call-done = bf16[1024,3584]{1,0:T(8,128)(2,1)} async-done(((bf16[32,3584]{1,0:T(8,128)(2,1)}), bf16[1024,3584]{1,0:T(8,128)(2,1)}) %all-gather.3.cloned.1.call-update) | async-done | bytes 7340048 | tf_op jit(solution)/shard_map/all_gather | solution.py:47
  107.9 6.1 fusion.80
  114.1 63.0 %all-reduce.4.cloned.1.call-done = f32[256,1024]{1,0:T(8,128)} async-done(((f32[256,1024]{1,0:T(8,128)}), f32[256,1024]{1,0:T(8,128)}) %all-reduce.4.cloned.1.call-update) | async-done | bytes 1048592 | tf_op jit(solution)/shard_map/psum | solution.py:51
  177.2 7.1 fusion.81
  188.1 159.2 %all-reduce.6.cloned.1.call-done = f32[1024,1024]{0,1:T(8,128)} async-done(((f32[1024,1024]{0,1:T(8,128)}), f32[1024,1024]{0,1:T(8,128)}) %all-reduce.6.cloned.1.call-update) | async-done | bytes 4194320 | tf_op jit(solution)/shard_map/psum | solution.py:52
  355.6 5.5 copy.7
  367.5 11.7 %cholesky.222 = f32[128,128]{1,0:T(8,128)S(1)} custom-call(f32[128,128]{1,0:T(8,128)S(1)} %cholesky.577), custom_call_target="Cholesky" | custom-call | tf_op jit(solution)/shard_map/jit(cholesky)/cholesky | solution.py:28
  379.3 9.8 custom-call.63
  392.2 11.7 %cholesky.243 = f32[128,128]{1,0:T(8,128)S(1)} custom-call(f32[128,128]{1,0:T(8,128)S(1)} %cholesky.581), custom_call_target="Cholesky" | custom-call | tf_op jit(solution)/shard_map/jit(cholesky)/cholesky | solution.py:28
  404.6 9.8 custom-call.64
  419.9 11.7 %cholesky.466 = f32[128,128]{1,0:T(8,128)S(1)} custom-call(f32[128,128]{1,0:T(8,128)S(1)} %cholesky.586), custom_call_target="Cholesky" | custom-call | tf_op jit(solution)/shard_map/jit(cholesky)/cholesky | solution.py:28
  432.4 9.8 custom-call.65
  447.0 11.7 %cholesky.485 = f32[128,128]{1,0:T(8,128)S(1)} custom-call(f32[128,128]{1,0:T(8,128)S(1)} %cholesky.591), custom_call_target="Cholesky" | custom-call | tf_op jit(solution)/shard_map/jit(cholesky)/cholesky | solution.py:28
  459.5 9.8 custom-call.66
  473.6 11.9 %cholesky.504 = f32[128,128]{1,0:T(8,128)S(1)} custom-call(f32[128,128]{1,0:T(8,128)S(1)} %cholesky.596), custom_call_target="Cholesky" | custom-call | tf_op jit(solution)/shard_map/jit(cholesky)/cholesky | solution.py:28
  486.2 9.8 custom-call.67
  500.4 11.7 %cholesky.524 = f32[128,128]{1,0:T(8,128)S(1)} custom-call(f32[128,128]{1,0:T(8,128)S(1)} %cholesky.601), custom_call_target="Cholesky" | custom-call | tf_op jit(solution)/shard_map/jit(cholesky)/cholesky | solution.py:28
  512.9 9.8 custom-call.68
  526.9 11.7 %cholesky.544 = f32[128,128]{1,0:T(8,128)S(1)} custom-call(f32[128,128]{1,0:T(8,128)S(1)} %cholesky.606), custom_call_target="Cholesky" | custom-call | tf_op jit(solution)/shard_map/jit(cholesky)/cholesky | solution.py:28
  539.4 9.8 custom-call.69
  552.3 11.7 %cholesky.562 = f32[128,128]{1,0:T(8,128)S(1)} custom-call(f32[128,128]{1,0:T(8,128)S(1)} %convolution_subtract_fusion.11), custom_call_target="Cholesky" | custom-call | tf_op jit(solution)/shard_map/jit(cholesky)/cholesky | solution.py:28
  574.4 4.9 select_select_fusion
  579.2 28.2 %while.1 = (s32[]{:T(128)}, f32[1024,1024]{0,1:T(8,128)}, s32[8,2]{0,1:T(2,128)S(1)}, f32[8,128,128]{2,1,0:T(8,128)}, s32[]{:T(128)}) while((s32[]{:T(128)}, f32[1024,1024]{0,1:T(8,128)}, s32[8,2]{0,1:T(2,128)S(1)}, f32[8,128,128]{2,1,0:T(8,128)}, s32[]{:T(128)}) %tuple.55), condition=%wide.while_cond, body=%wide.while_body.sunk | while | flops 2 | bytes 393829 | solution.py:29
  607.5 79.6 %custom-call.70 = f32[8,128,128]{1,2,0:T(8,128)S(1)} custom-call(f32[8,128,128]{2,1,0:T(8,128)} %get-tuple-element.10), custom_call_target="InvertDiagBlocksLowerTriangular" | custom-call | tf_op jit(solution)/shard_map/jit(_solve_triangular)/triangular_solve | solution.py:29
  704.6 5.6 convolution_subtract_fusion.2
  710.9 6.1 convolution_subtract_fusion.1
  717.7 7.5 convolution_subtract_fusion.3
  729.7 5.1 convolution_convert_fusion
  734.8 222.5 %reduce-scatter.2.cloned.1.call-done = bf16[32,3584]{1,0:T(8,128)(2,1)} async-done(((bf16[1024,3584]{1,0:T(8,128)(2,1)}), bf16[32,3584]{1,0:T(8,128)(2,1)}) %reduce-scatter.2.cloned.1.call-update) | async-done | bytes 229392 | tf_op jit(solution)/shard_map/reduce_scatter | solution.py:56
  958.7 78.8 %psum.23 = f32[1024]{0:T(1024)S(1)} all-reduce(f32[1024]{0:T(1024)S(1)} %dynamic_update_slice.3), channel_id=1, replica_groups=mesh['dp'=32,'tensor'=8] {'dp','tensor'}, use_global_device_ids=true, to_apply=%region_21.22 | all-reduce | flops 1024 | bytes 8192 | tf_op jit(solution)/shard_map/psum | solution.py:69
  1039.5 15.7 %all-gather.5.cloned.1.call-done = bf16[1024,3584]{1,0:T(8,128)(2,1)} async-done(((bf16[32,3584]{1,0:T(8,128)(2,1)}), bf16[1024,3584]{1,0:T(8,128)(2,1)}) %all-gather.5.cloned.1.call-update) | async-done | bytes 7340048 | tf_op jit(solution)/shard_map/all_gather | solution.py:75
  1055.2 6.2 fusion.28
  (144 shorter events, 119.4 us)
Async XLA Ops:
  7.2 100.7 %all-gather.3.cloned.1.call-start = ((), (), s32[]{:S(2)}) async-start(), calls=%async_computation.1 | async-start | bytes 7569408 | tf_op jit(solution)/shard_map/all_gather | solution.py:47
  9.0 168.2 %all-reduce.4.cloned.1.call-start = ((), (), s32[]{:S(2)}) async-start(), calls=%async_computation.2 | async-start | bytes 2097152 | tf_op jit(solution)/shard_map/psum | solution.py:51
  114.1 233.2 %all-reduce.6.cloned.1.call-start = ((), (), s32[]{:S(2)}) async-start(), calls=%async_computation.3 | async-start | bytes 8388608 | tf_op jit(solution)/shard_map/psum | solution.py:52
  184.3 773.0 %reduce-scatter.2.cloned.1.call-start = ((), (), s32[]{:S(2)}) async-start(), calls=%async_computation.4 | async-start | bytes 7569408 | tf_op jit(solution)/shard_map/reduce_scatter | solution.py:56
  365.6 2.0 copy-start.2
  415.5 2.0 copy-start
  687.0 4.4 copy-start.1
  717.0 8.9 copy-start.3
  734.8 320.4 %all-gather.5.cloned.1.call-start = ((), (), s32[]{:S(2)}) async-start(), calls=%async_computation.5 | async-start | bytes 7569408 | tf_op jit(solution)/shard_map/all_gather | solution.py:75
Sparse Core Ops, SparseCore 0:
  11.1 96.7 all-gather.2
  114.2 62.9 all-reduce.3
  184.4 162.8 all-reduce.5
  734.9 222.3 reduce-scatter.1
  959.7 95.4 all-gather.4
where the time goes:
time: 1080 us; the launch traced here: 1070 us
  waiting for transfers between devices  557 us (52%)
  other arithmetic  277 us (26%)
  matrix products  93.6 us (9%)
  blocking collectives  78.8 us (7%)
  local copies, waits for them, and re-layouts  44.9 us (4%)
  between operations  20 us (2%)
    reduce_scatter x1, waiting for transfers between devices, per_device(): lax.psum_scatter(lax.dot_general(orthonormal, summed, (((0,), (0,)), ((),...  222 us
    another operation x30, other arithmetic, inverse_factor(): lower_factor = jnp.linalg.cholesky(shifted)  167 us
    psum x1, waiting for transfers between devices, per_device(): gram_matrix = lax.psum(gram_of(sketch), 'dp')  159 us
    all_gather x1, waiting for transfers between devices, per_device(): full_basis = lax.all_gather(narrow_basis, 'dp', axis=0, tiled=True)  96.4 us
    another operation x3, other arithmetic, inverse_factor(): return jax.scipy.linalg.solve_triangular(lower_factor, identity, lower=True)  84.4 us
    psum x1, blocking collectives, per_device(): column_norms = jnp.sqrt(lax.psum(placed, ('dp', 'tensor'))) + NORM_EPS  78.8 us
    psum x1, waiting for transfers between devices, per_device(): sketch = lax.psum(partial_sketch, 'tensor')  63 us
    another operation x15, matrix products, inverse_factor(): return jax.scipy.linalg.solve_triangular(lower_factor, identity, lower=True)  38.7 us
  transfers between devices with their start and end apart: 5, of which 5 were waited for; matrix products, arithmetic and copies ran while one was open for 1% of the time, Pallas kernels for 0%

commit v1 on v0

v1 whole, which is shorter than its diff:
```python
import functools
import math

import jax
import jax.numpy as jnp
from jax import lax
from jax.experimental import pallas as pl
from jax.experimental.pallas import tpu as pltpu
from jax.sharding import Mesh, PartitionSpec as P

D = 8192
FF = 28672
R = 1024
MOMENTUM = 0.95
JITTER = 0.001
NORM_EPS = 1e-08

DP = ("y", "z")
TENSOR = ("x", "c")
HIGHEST = lax.Precision.HIGHEST
BLOCK = 128


def dot_tn(a, b):
    return lax.dot_general(
        a, b, (((0,), (0,)), ((), ())), precision=HIGHEST, preferred_element_type=jnp.float32
    )


def dot_nn(a, b):
    return lax.dot_general(
        a, b, (((1,), (0,)), ((), ())), precision=HIGHEST, preferred_element_type=jnp.float32
    )


def spread(row):
    return jnp.broadcast_to(row, (8, BLOCK))


def factor_block(a_ref, x_ref):
    rows = lax.broadcasted_iota(jnp.int32, (8, BLOCK), 0)
    for panel in range(BLOCK // 8):
        top = 8 * panel
        a_rows = a_ref[top : top + 8, :]
        x_rows = x_ref[top : top + 8, :]
        pivots = [spread(a_rows[:, top + c : top + c + 1]) for c in range(8)]
        scale = jnp.ones((8, BLOCK), jnp.float32)
        for c in range(8):
            pivot = spread(pivots[c][c : c + 1, :])
            scale = jnp.where(rows == c, lax.rsqrt(pivot), scale)
            if c < 7:
                factor = jnp.where(rows > c, pivots[c] * (1.0 / pivot), 0.0)
                for later in range(c + 1, 8):
                    pivots[later] = pivots[later] - factor * spread(pivots[later][c : c + 1, :])
                a_rows = a_rows - factor * spread(a_rows[c : c + 1, :])
                x_rows = x_rows - factor * spread(x_rows[c : c + 1, :])
        a_rows = a_rows * scale
        x_rows = x_rows * scale
        x_ref[top : top + 8, :] = x_rows
        if panel < BLOCK // 8 - 1:
            columns = a_rows.T
            a_spread = [spread(a_rows[c : c + 1, :]) for c in range(8)]
            x_spread = [spread(x_rows[c : c + 1, :]) for c in range(8)]
            for tile in range(panel + 1, BLOCK // 8):
                at = 8 * tile
                a_tile = a_ref[at : at + 8, :]
                x_tile = x_ref[at : at + 8, :]
                for c in range(8):
                    factor = spread(columns[at : at + 8, c : c + 1])
                    a_tile = a_tile - factor * a_spread[c]
                    x_tile = x_tile - factor * x_spread[c]
                a_ref[at : at + 8, :] = a_tile
                x_ref[at : at + 8, :] = x_tile


def inverse_factor_kernel(size, gram_ref, out_ref, upper, panel_a, panel_x, a_ref, x_ref, shift_ref):
    blocks = size // BLOCK
    shape = (BLOCK, BLOCK)
    eye = lax.broadcasted_iota(jnp.int32, shape, 0) == lax.broadcasted_iota(jnp.int32, shape, 1)
    diagonal = jnp.zeros(shape, jnp.float32)
    for k in range(blocks):
        at = BLOCK * k
        diagonal = diagonal + jnp.where(eye, gram_ref[at : at + BLOCK, at : at + BLOCK], 0.0)
    trace = jnp.sum(jnp.sum(diagonal, axis=1, keepdims=True), axis=0, keepdims=True)
    shift_ref[...] = jnp.where(eye, jnp.broadcast_to(trace * (JITTER / size), shape), 0.0)
    out_ref[...] = jnp.zeros_like(out_ref)

    def step(k, carry):
        for at in range(0, size, BLOCK):

            @pl.when(k == at // BLOCK)
            def _(at=at):
                if at == 0:
                    panel_a[:, :] = gram_ref[0:BLOCK, :]
                    a_ref[...] = gram_ref[0:BLOCK, 0:BLOCK] + shift_ref[...]
                else:
                    above = upper[0:at, at : at + BLOCK]
                    reduced = gram_ref[at : at + BLOCK, at:] - dot_tn(above, upper[0:at, at:])
                    panel_a[:, at:] = reduced
                    a_ref[...] = reduced[:, :BLOCK] + shift_ref[...]
                    panel_x[:, 0:at] = -dot_tn(above, out_ref[0:at, 0:at])

        x_ref[...] = jnp.where(eye, 1.0, 0.0)
        factor_block(a_ref, x_ref)
        for at in range(0, size, BLOCK):

            @pl.when(k == at // BLOCK)
            def _(at=at):
                own = x_ref[...]
                if at + BLOCK < size:
                    upper[at : at + BLOCK, at + BLOCK :] = dot_nn(own, panel_a[:, at + BLOCK :])
                if at > 0:
                    out_ref[at : at + BLOCK, 0:at] = dot_nn(own, panel_x[:, 0:at])
                out_ref[at : at + BLOCK, at : at + BLOCK] = own

        return carry

    lax.fori_loop(0, blocks, step, 0)


def inverse_factor(gram_matrix):
    size = gram_matrix.shape[0]
    return pl.pallas_call(
        functools.partial(inverse_factor_kernel, size),
        out_shape=jax.ShapeDtypeStruct((size, size), jnp.float32),
        in_specs=[pl.BlockSpec(memory_space=pltpu.VMEM)],
        out_specs=pl.BlockSpec(memory_space=pltpu.VMEM),
        scratch_shapes=[
            pltpu.VMEM((size, size), jnp.float32),
            pltpu.VMEM((BLOCK, size), jnp.float32),
            pltpu.VMEM((BLOCK, size), jnp.float32),
            pltpu.VMEM((BLOCK, BLOCK), jnp.float32),
            pltpu.VMEM((BLOCK, BLOCK), jnp.float32),
            pltpu.VMEM((BLOCK, BLOCK), jnp.float32),
        ],
        compiler_params=pltpu.CompilerParams(vmem_limit_bytes=32 * 2**20),
        cost_estimate=pl.CostEstimate(
            flops=60_000_000_000, bytes_accessed=8 * 2**20, transcendentals=0
        ),
    )(gram_matrix)


def halves_psum(array, axes):
    middle = array.shape[0] // 2
    return jnp.concatenate(lax.psum((array[:middle], array[middle:]), axes), axis=0)


def per_device(momentum, grad, basis):
    summed = (momentum.astype(jnp.float32) + grad.astype(jnp.float32)).astype(jnp.bfloat16)
    summed = lax.optimization_barrier(summed)
    narrow_basis = basis.astype(jnp.bfloat16)
    rank_rows = basis.shape[0]
    full_basis = lax.all_gather(narrow_basis, DP, axis=0, tiled=True)
    partial_sketch = lax.dot_general(
        summed, full_basis, (((1,), (1,)), ((), ())), preferred_element_type=jnp.float32
    )
    sketch = halves_psum(partial_sketch, TENSOR)
    gram_matrix = halves_psum(dot_tn(sketch, sketch), DP)
    inverse = inverse_factor(gram_matrix)
    orthonormal = lax.dot_general(
        sketch,
        inverse,
        (((1,), (1,)), ((), ())),
        precision=HIGHEST,
        preferred_element_type=jnp.float32,
    ).astype(jnp.bfloat16)
    partial_coefficients = lax.dot_general(
        orthonormal, summed, (((0,), (0,)), ((), ())), preferred_element_type=jnp.float32
    ).astype(jnp.bfloat16)
    coefficients = halves_psum(partial_coefficients, DP)
    wide = coefficients.astype(jnp.float32)
    column_norms = jnp.sqrt(lax.psum(jnp.sum(wide * wide, axis=1), TENSOR)) + NORM_EPS
    scaling = math.sqrt(D * FF / R) / column_norms
    scaled = (orthonormal.astype(jnp.float32) * scaling[None, :]).astype(jnp.bfloat16)
    feedback = jnp.dot(orthonormal, coefficients, preferred_element_type=jnp.float32)
    new_momentum = (summed.astype(jnp.float32) - (1.0 - MOMENTUM) * feedback).astype(jnp.bfloat16)
    update = jnp.dot(scaled, coefficients, preferred_element_type=jnp.float32).astype(jnp.bfloat16)
    own_start = lax.axis_index(DP) * rank_rows
    own = lax.dynamic_slice_in_dim(coefficients, own_start, rank_rows, 0).astype(jnp.float32)
    own_norms = lax.dynamic_slice_in_dim(column_norms, own_start, rank_rows, 0)
    new_basis = math.sqrt(FF) * own / own_norms[:, None]
    return (update, new_momentum, new_basis)


def solution(mesh):
    split = Mesh(mesh.devices.reshape(4, 8, 4, 2), ("y", "z", "x", "c"))
    spec = P(DP, TENSOR)
    return jax.shard_map(
        per_device, mesh=split, in_specs=(spec,) * 3, out_specs=(spec,) * 3, check_vma=False
    )
```

time: 1080 us -> 657 us (0.61)
  other arithmetic: 277 us -> 10.3 us
  matrix products: 93.6 us -> 24.1 us
  blocking collectives: 78.8 us -> 12.4 us
  Pallas kernels: 0 us -> 59.5 us
  waiting for transfers between devices: 557 us -> 521 us
  local copies, waits for them, and re-layouts: 44.9 us -> 13.8 us
    another operation x33 -> x0, other arithmetic: 252 us -> none  [the longest x30 167 us: inverse_factor(): lower_factor = jnp.linalg.cholesky(shifted)]
    reduce_scatter x1 -> x0, waiting for transfers between devices: 222 us -> none  [per_device(): lax.psum_scatter(lax.dot_general(orthonormal, summed, (((0,), (0,)), ((),...]
    psum x2 -> x3, waiting for transfers between devices: 222 us -> 425 us  [halves_psum(): lax.psum((array[:middle], array[middle:]), axes)]
    psum x1, blocking collectives: 78.8 us -> 12.4 us  [per_device(): lax.psum(jnp.sum(wide * wide, axis=1), TENSOR)]
    another operation x29 -> x0, matrix products: 65.4 us -> none  [the longest x15 38.7 us: inverse_factor(): return jax.scipy.linalg.solve_triangular(lower_factor, identity, lower=True)]
    pallas_call x0 -> x1, Pallas kernels: none -> 59.5 us  [inverse_factor(): pl.pallas_call(functools.partial(inverse_factor_kernel, size), out_shape=...]
    another operation x66 -> x0, local copies, waits for them, and re-layouts: 33.7 us -> none
    all_gather x2 -> x1, waiting for transfers between devices: 112 us -> 96.4 us  [per_device(): full_basis = lax.all_gather(narrow_basis, DP, axis=0, tiled=True)]
  transfers between devices with their start and end apart: 5 -> 4, of which waited for: 5 -> 4; matrix products, arithmetic and copies ran while one was open for 1% -> 0% of each run, Pallas kernels for 0% -> 0%
where the time goes in v1:
time: 657 us; the launch traced here: 655 us
  waiting for transfers between devices  521 us (79%)
  Pallas kernels  59.5 us (9%)
  matrix products  24.1 us (4%)
  local copies, waits for them, and re-layouts  13.8 us (2%)
  between operations  13.8 us (2%)
  blocking collectives  12.4 us (2%)
  other arithmetic  10.3 us (2%)
    psum x3, waiting for transfers between devices, halves_psum(): lax.psum((array[:middle], array[middle:]), axes)  425 us
    all_gather x1, waiting for transfers between devices, per_device(): full_basis = lax.all_gather(narrow_basis, DP, axis=0, tiled=True)  96.4 us
    pallas_call x1, Pallas kernels, inverse_factor(): pl.pallas_call(functools.partial(inverse_factor_kernel, size), out_shape=...  59.5 us
  transfers between devices with their start and end apart: 4, of which 4 were waited for; matrix products, arithmetic and copies ran while one was open for 0% of the time, Pallas kernels for 0%

profile of v1, /device:TPU:1, one launch (start us, length us, event | category | flops | bytes accessed | tf_op | source)
XLA Modules:
  0.0 655.4 jit_solution(755115066920982333)
XLA Ops:
  7.2 0.0 all-gather.2.cloned.1.call-start
  7.2 1.7 convert_element_type.42
  8.9 0.0 all-gather.2.cloned.1.call-update
  9.0 0.0 all-reduce.9.cloned.1.call-start
  9.0 2.5 add_convert_fusion
  11.5 96.4 %all-gather.2.cloned.1.call-done = bf16[1024,3584]{1,0:T(8,128)(2,1)} async-done(((bf16[32,3584]{1,0:T(8,128)(2,1)}), bf16[1024,3584]{1,0:T(8,128)(2,1)}) %all-gather.2.cloned.1.call-update) | async-done | bytes 7340048 | tf_op jit(solution)/shard_map/all_gather | solution.py:153
  107.9 5.2 fusion.6
  113.1 1.0 fusion.5
  114.1 0.0 all-reduce.7.cloned.1.call-start
  114.2 63.3 %all-reduce.9.cloned.1.call-done = (f32[128,1024]{1,0:T(8,128)}, f32[128,1024]{1,0:T(8,128)}) async-done(((f32[128,1024]{1,0:T(8,128)}, f32[128,1024]{1,0:T(8,128)}), (f32[128,1024]{1,0:T(8,128)}, f32[128,1024]{1,0:T(8,128)})) %all-reduce.9.cloned.1.call-update) | async-done | bytes 1048592 | tf_op jit(solution)/shard_map/psum | solution.py:145
  177.5 1.1 constant_dynamic-update-slice_fusion.1
  178.5 1.1 constant_dynamic-update-slice_fusion
  179.6 3.5 fusion.7
  183.1 2.3 fusion.4
  185.4 0.0 all-reduce.11.cloned.1.call-start
  185.5 163.4 %all-reduce.7.cloned.1.call-done = (f32[512,1024]{1,0:T(8,128)}, f32[512,1024]{1,0:T(8,128)}) async-done(((f32[512,1024]{1,0:T(8,128)}, f32[512,1024]{1,0:T(8,128)}), (f32[512,1024]{1,0:T(8,128)}, f32[512,1024]{1,0:T(8,128)})) %all-reduce.7.cloned.1.call-update) | async-done | bytes 4194320 | tf_op jit(solution)/shard_map/psum | solution.py:145
  348.9 2.8 pad_maximum_fusion.gram_ref
  351.7 59.5 %shard_map.58 = f32[1024,1024]{1,0:T(8,128)S(1)} custom-call(f32[1024,1024]{1,0:T(8,128)S(1)} %pad_maximum_fusion.gram_ref), custom_call_target="tpu_custom_call" | custom-call | flops 60000002048 | bytes 8388608 | tf_op jit(solution)/shard_map/pallas_call | solution.py:123
  411.1 3.7 convolution_convert_fusion.2
  414.8 2.1 convolution_convert_fusion
  417.0 3.5 fusion.3
  420.5 198.1 %all-reduce.11.cloned.1.call-done = (bf16[512,3584]{1,0:T(8,128)(2,1)}, bf16[512,3584]{1,0:T(8,128)(2,1)}) async-done(((bf16[512,3584]{1,0:T(8,128)(2,1)}, bf16[512,3584]{1,0:T(8,128)(2,1)}), (bf16[512,3584]{1,0:T(8,128)(2,1)}, bf16[512,3584]{1,0:T(8,128)(2,1)})) %all-reduce.11.cloned.1.call-update) | async-done | bytes 7340048 | tf_op jit(solution)/shard_map/psum | solution.py:145
  618.6 2.4 constant_dynamic-update-slice_fusion.3
  621.0 0.7 copy-done.1
  621.7 0.2 constant_dynamic-update-slice_fusion.2
  622.0 1.5 multiply_reduce_fusion
  623.5 1.4 copy-done
  624.9 3.3 fusion.1
  628.2 12.4 %psum.55 = f32[1024]{0:T(1024)S(1)} all-reduce(f32[1024]{0:T(1024)S(1)} %multiply_reduce_fusion), channel_id=1, replica_groups=mesh['y'=4,'z'=8,'x'=4,'c'=2] {'x','c'}, use_global_device_ids=true, to_apply=%region_7.0 | all-reduce | flops 1024 | bytes 8192 | tf_op jit(solution)/shard_map/psum | solution.py:172
  640.6 0.1 dynamic_slice.7
  640.7 1.8 multiply_divide_fusion
  642.5 6.4 convolution_convert_fusion.1
  (6 shorter events, 0.1 us)
Async XLA Ops:
  7.2 100.7 %all-gather.2.cloned.1.call-start = ((), (), s32[]{:S(2)}) async-start(), calls=%async_computation | async-start | bytes 7569408 | tf_op jit(solution)/shard_map/all_gather | solution.py:153
  9.0 168.5 %all-reduce.9.cloned.1.call-start = ((), (), s32[]{:S(2)}) async-start(), calls=%async_computation.2 | async-start | bytes 2097152 | tf_op jit(solution)/shard_map/psum | solution.py:145
  114.1 234.7 %all-reduce.7.cloned.1.call-start = ((), (), s32[]{:S(2)}) async-start(), calls=%async_computation.1 | async-start | bytes 8388608 | tf_op jit(solution)/shard_map/psum | solution.py:145
  185.4 433.1 %all-reduce.11.cloned.1.call-start = ((), (), s32[]{:S(2)}) async-start(), calls=%async_computation.3 | async-start | bytes 14680064 | tf_op jit(solution)/shard_map/psum | solution.py:145
  618.6 3.1 copy-start.1
  622.0 2.9 copy-start
Sparse Core Ops, SparseCore 0:
  11.2 96.7 all-gather.1
  114.3 63.1 all-reduce.8
  185.6 163.2 all-reduce.6
  420.6 197.9 all-reduce.10
